TPU v7x, 256 devices: a whole 4x4x8 slice. The times are simulated.
256 devices in a mesh: row: 8 (over x, core), col: 32 (over z, y).
Axes of the slice: x: 4, y: 4, z: 8, core: 2. Of those that a mesh axis runs over, the one named last changes fastest.
Arguments:
- matrix: bfloat16 [16384, 65536], P('row', 'col'), may hold values from -8 to 8
- basis: bfloat16 [16384, 256], P(('row', 'col')), may hold values from -110 to 110
Outputs:
- orthobasis: float32 [16384, 256], P(('row', 'col'))
- triangle: float32 [256, 256], replicated
All inputs are finite; a program needn't handle non-finite values.
Results may differ from a plain program's by a relative error of at most 0.0018.
Values may be sent and summed in bfloat16 or wider, within the bound.
A program may use at most 64 MiB of HBM per device.

v0:
```python
import jax
import jax.numpy as jnp
from jax import lax
from jax.sharding import PartitionSpec as P


def body(matrix, basis):
    rows_dev, cols_dev = matrix.shape
    total_rows = rows_dev * lax.axis_size("row")
    total_cols = cols_dev * lax.axis_size("col")
    partial_value = lax.dot_general(
        matrix,
        lax.all_gather(basis, "col", axis=0, tiled=True),
        (((0,), (0,)), ((), ())),
        preferred_element_type=jnp.float32,
    )
    sketch = (lax.psum(partial_value, "row") * total_rows ** (-0.5)).astype(jnp.bfloat16)
    image_part = jnp.dot(matrix, sketch, preferred_element_type=jnp.float32)
    highest = lax.Precision.HIGHEST
    owned = lax.psum_scatter(image_part, "col", scatter_dimension=0, tiled=True) * total_cols ** (
        -0.5
    )
    local_gram = jnp.dot(owned.T, owned, precision=highest) / total_rows
    lower = jnp.linalg.cholesky(lax.psum(local_gram, ("row", "col")))
    orthobasis = jax.scipy.linalg.solve_triangular(lower, owned.T, lower=True).T
    return (orthobasis, lower.T)


def solution(mesh):
    in_specs = (P("row", "col"), P(("row", "col"), None))
    out_specs = (P(("row", "col"), None), P())
    return jax.shard_map(body, mesh=mesh, in_specs=in_specs, out_specs=out_specs, check_vma=False)
```

profile of v0, /device:TPU:1, one launch (start us, length us, event | category | flops | bytes accessed | tf_op | source)
XLA Modules:
  0.0 715.5 jit_solution(12563164536958644333)
XLA Ops:
  7.2 0.0 all-gather.2.cloned.1.call-start
  7.2 0.7 all-gather.2.cloned.1.call-update
  7.9 0.0 all-reduce.4.cloned.1.call-start
  7.9 78.3 %all-gather.2.cloned.1.call-done = bf16[2048,256]{1,0:T(8,128)(2,1)} async-done(((bf16[64,256]{1,0:T(8,128)(2,1)}), bf16[2048,256]{1,0:T(8,128)(2,1)}) %all-gather.2.cloned.1.call-update) | async-done | bytes 1048592 | tf_op jit(solution)/shard_map/all_gather | solution.py:13
  86.2 7.4 %fusion.16 = f32[2048,256]{1,0:T(8,128)} fusion(bf16[2048,2048]{1,0:T(8,128)(2,1)} %param.2, bf16[2048,256]{1,0:T(8,128)(2,1)} %all-gather.2.cloned.1.call-done), kind=kOutput, calls=%fused_computation.40 | convolution fusion | flops 2147483648 | bytes 11534336 | tf_op jit(solution)/shard_map/dot_general | solution.py:11
  93.7 0.0 all-reduce.4.cloned.1.call-update
  93.7 0.0 reduce-scatter.4.cloned.1.call-start
  93.7 70.9 %all-reduce.4.cloned.1.call-done = f32[2048,256]{1,0:T(8,128)} async-done(((f32[2048,256]{1,0:T(8,128)}), f32[2048,256]{1,0:T(8,128)}) %all-reduce.4.cloned.1.call-update) | async-done | bytes 2097168 | tf_op jit(solution)/shard_map/psum | solution.py:17
  164.6 6.4 convolution_bitcast_fusion
  171.0 1.9 copy.11
  172.9 0.0 reduce-scatter.4.cloned.1.call-update
  172.9 0.2 all-reduce.6.cloned.1.call-start
  173.2 212.6 %reduce-scatter.4.cloned.1.call-done = f32[64,256]{1,0:T(8,128)} async-done(((f32[2048,256]{1,0:T(8,128)}), f32[64,256]{1,0:T(8,128)}) %reduce-scatter.4.cloned.1.call-update) | async-done | bytes 65552
  385.8 0.9 copy.12
  386.7 1.1 convolution_multiply_fusion
  387.8 0.0 all-reduce.6.cloned.1.call-update
  387.9 256.8 %all-reduce.6.cloned.1.call-done = f32[256,256]{0,1:T(8,128)} async-done(((f32[256,256]{0,1:T(8,128)}), f32[256,256]{0,1:T(8,128)}) %all-reduce.6.cloned.1.call-update) | async-done | bytes 262160 | tf_op jit(solution)/shard_map/psum | solution.py:24
  644.7 1.1 copy.8
  645.8 1.0 fusion.1
  646.8 11.7 %cholesky.50 = f32[128,128]{1,0:T(8,128)S(1)} custom-call(f32[128,128]{1,0:T(8,128)S(1)} %cholesky.118), custom_call_target="Cholesky" | custom-call | tf_op jit(solution)/shard_map/jit(cholesky)/cholesky | solution.py:24
  658.5 9.8 %custom-call.15 = f32[1,128,128]{1,2,0:T(8,128)S(1)} custom-call(f32[1,128,128]{2,1,0:T(8,128)S(1)} %get-tuple-element.29), custom_call_target="InvertDiagBlocksLowerTriangular" | custom-call | tf_op jit(solution)/shard_map/jit(cholesky)/cholesky | solution.py:24
  668.4 0.2 constant_dynamic-update-slice_fusion.1
  668.6 0.3 convolution_subtract_fusion.1
  668.8 11.7 %cholesky.105 = f32[128,128]{1,0:T(8,128)S(1)} custom-call(f32[128,128]{1,0:T(8,128)S(1)} %convolution_subtract_fusion.1), custom_call_target="Cholesky" | custom-call | tf_op jit(solution)/shard_map/jit(cholesky)/cholesky | solution.py:24
  680.6 0.7 compare_reduce_fusion
  682.7 0.1 triangular_solve.57
  682.8 4.3 while.1
  683.0 0.6 fusion.25
  683.6 1.4 bitcast_dynamic-update-slice_fusion.2
  685.0 0.6 fusion.25
  685.6 1.4 bitcast_dynamic-update-slice_fusion.2
  687.1 19.7 %custom-call.16 = f32[2,128,128]{1,2,0:T(8,128)S(1)} custom-call(f32[2,128,128]{2,1,0:T(8,128)S(1)} %get-tuple-element.9), custom_call_target="InvertDiagBlocksLowerTriangular" | custom-call | tf_op jit(solution)/shard_map/jit(_solve_triangular)/triangular_solve | solution.py:25
  706.7 0.3 fusion.7
  707.0 0.2 convolution_subtract_fusion
  707.2 0.3 fusion.6
  707.5 0.6 maximum_bitcast_fusion
  708.1 0.8 copy.9
  (10 shorter events, 0.2 us)
Async XLA Ops:
  7.2 79.1 %all-gather.2.cloned.1.call-start = ((), (), s32[]{:S(2)}) async-start(), calls=%async_computation.1 | async-start | bytes 1081344 | tf_op jit(solution)/shard_map/all_gather | solution.py:13
  7.9 156.7 %all-reduce.4.cloned.1.call-start = ((), (), s32[]{:S(2)}) async-start(), calls=%async_computation.2 | async-start | bytes 4194304 | tf_op jit(solution)/shard_map/psum | solution.py:17
  93.7 292.1 %reduce-scatter.4.cloned.1.call-start = ((), (), s32[]{:S(2)}) async-start(), calls=%async_computation.4 | async-start | bytes 2162688
  172.9 471.7 %all-reduce.6.cloned.1.call-start = ((), (), s32[]{:S(2)}) async-start(), calls=%async_computation.3 | async-start | bytes 524288 | tf_op jit(solution)/shard_map/psum | solution.py:24
Sparse Core Ops, SparseCore 0:
  10.6 75.6 all-gather.1
  93.8 70.7 all-reduce.3
  173.1 212.6 reduce-scatter.3
  392.6 252.0 all-reduce.5
where the time goes:
time: 716 us
  waiting for transfers between devices  619 us (86%)
  other arithmetic  55.4 us (8%)
  matrix products  16.2 us (2%)
  between operations  15.2 us (2%)
  local copies, waits for them, and re-layouts  8.87 us (1%)
    psum x1, waiting for transfers between devices, body(): lower = jnp.linalg.cholesky(lax.psum(local_gram, ('row', 'col')))  257 us
    unnamed x5, waiting for transfers between devices  213 us
    all_gather x1, waiting for transfers between devices, body(): lax.all_gather(basis, 'col', axis=0, tiled=True)  78.3 us
    psum x1, waiting for transfers between devices, body(): lax.psum(partial_value, 'row') * total_rows ** (-0.5)  70.9 us
    another operation x6, other arithmetic, body(): lower = jnp.linalg.cholesky(lax.psum(local_gram, ('row', 'col')))  34 us
    another operation x2, other arithmetic, body(): orthobasis = jax.scipy.linalg.solve_triangular(lower, owned.T, lower=True).T  19.7 us
  transfers between devices with their start and end apart: 4, of which 4 were waited for; matrix products, arithmetic and copies ran while one was open for 0% of the time, Pallas kernels for 0%

commit v1 on v0

v1 whole, which is shorter than its diff:
```python
import functools

import jax
import jax.numpy as jnp
from jax import lax
from jax.experimental import pallas as pl
from jax.experimental.pallas import tpu as pltpu
from jax.sharding import PartitionSpec as P

F32 = jnp.float32
BF16 = jnp.bfloat16
NX, NY, NZ = 4, 4, 8
KC = 256
BLK = 64
GA = 48
IA = 48
IDT = BF16
XS = (2, 1, 3, 0)


def kernel(
    a_hbm, basis, img_out, gram_out,
    av, g, bt, part, rk, own, xs, xr, st, im, sa, sb, ya, zb, ta, ub, za, yb,
    g0, gk, g1, gx, g2, gy, gz, gf,
    asem, s_gz, r_gz, s_gzy, r_gzy, s_gy, r_gy, s_gyz, r_gyz,
    s_k, r_k, s_x, r_x, s_sx, r_sx, s_sk, r_sk,
    s_ya, r_ya, s_zb, r_zb, s_za, r_za, s_yb, r_yb,
    s_q, r_q,
):
    r = lax.axis_index("row")
    c = lax.axis_index("col")
    x, k = r // 2, r % 2
    z, y = c // NY, c % NY

    def at_x(s):
        return (((x + s) % NX) * 2 + k, c)

    def at_k():
        return (x * 2 + 1 - k, c)

    def at_y(s):
        return (r, z * NY + (y + s) % NY)

    def at_z(s):
        return (r, ((z + s) % NZ) * NY + y)

    loads = []
    for j in range(8):
        cp = pltpu.make_async_copy(a_hbm.at[:, pl.ds(256 * j, 256)], av.at[j], asem.at[j])
        cp.start()
        loads.append(cp)

    barrier = pltpu.get_barrier_semaphore()
    for s in range(1, NZ):
        pl.semaphore_signal(barrier, 1, device_id=at_z(s))
    for s in range(1, NY):
        pl.semaphore_signal(barrier, 1, device_id=at_y(s))
    for s in range(1, NX):
        pl.semaphore_signal(barrier, 1, device_id=at_x(s))
    pl.semaphore_signal(barrier, 1, device_id=at_k())
    g[z, y] = basis[...]
    pl.semaphore_wait(barrier, NZ + NY + NX - 3 + 1)

    sends = []

    def copy(src, dst, ss, rs, dev):
        cp = pltpu.make_async_remote_copy(src, dst, ss, rs, device_id=dev)
        cp.start()
        sends.append(cp)
        return cp

    hi, lo = pl.ds(0, GA), pl.ds(GA, BLK - GA)
    zorder = (1, 7, 2, 6, 3, 5, 4)
    cy = {s: copy(basis.at[lo], g.at[z, y, lo], s_gy.at[s], r_gy.at[s], at_y(s)) for s in (2, 1, 3)}
    cz = {s: copy(basis.at[hi], g.at[z, y, hi], s_gz.at[s], r_gz.at[s], at_z(s)) for s in zorder}
    czy = {}
    for t in (2, 1, 3):
        czy[0, t] = copy(basis.at[hi], g.at[z, y, hi], s_gzy.at[0, t], r_gzy.at[0, t], at_y(t))
    for s in (1, 3, 2):
        cy[s].wait_recv()
    cyz = {}
    for s in (4, 3, 5, 2, 6, 1, 7):
        cyz[s] = copy(g.at[z, :, lo], g.at[z, :, lo], s_gyz.at[s], r_gyz.at[s], at_z(s))
    for s in zorder:
        cz[s].wait_recv()
        zs = (z + NZ - s) % NZ
        for t in (2, 1, 3):
            czy[s, t] = copy(
                g.at[zs, y, hi], g.at[zs, y, hi], s_gzy.at[s, t], r_gzy.at[s, t], at_y(t)
            )
    for cp in cyz.values():
        cp.wait_recv()
    for cp in czy.values():
        cp.wait_recv()

    def turn(i, carry):
        bt[:, pl.ds(pl.multiple_of(i * 256, 256), 256)] = g[i].reshape(NY * BLK, KC).T
        return carry

    lax.fori_loop(0, NZ, turn, 0)
    for cp in loads:
        cp.wait()

    def product(j):
        return jnp.dot(bt[...], av[j], preferred_element_type=F32)

    ck = []
    for i, s in enumerate(XS):
        part[i] = product(2 * ((x + s) % NX) + 1 - k)
        ck.append(copy(part.at[i], rk.at[i], s_k.at[i], r_k.at[i], at_k()))
    cx = []
    for i, s in enumerate(XS):
        p = product(2 * ((x + s) % NX) + k)
        ck[i].wait_recv()
        p = p + rk[i]
        if s:
            xs[i] = p
            cx.append(copy(xs.at[i], xr.at[i], s_x.at[i], r_x.at[i], at_x(s)))
        else:
            own[...] = p
    for cp in cx:
        cp.wait_recv()
    total = (own[...] + xr[0]) + (xr[1] + xr[2])
    st[r] = (total * (16384.0**-0.5)).astype(BF16)
    csx = {}
    csk = {0: copy(st.at[r], st.at[r], s_sk.at[0], r_sk.at[0], at_k())}
    for s in (2, 1, 3):
        csx[s] = copy(st.at[r], st.at[r], s_sx.at[s], r_sx.at[s], at_x(s))

    def add(ja, jb, first, last):
        def tile(i, carry):
            zi = i
            rows = pl.ds(pl.multiple_of(i * 256, 256), 256)
            v = lax.dot_general(av[ja, rows, :], st[ja], (((1,), (1,)), ((), ())), preferred_element_type=F32)
            v += lax.dot_general(av[jb, rows, :], st[jb], (((1,), (1,)), ((), ())), preferred_element_type=F32)
            if not first:
                v += im[rows, :]
            im[rows, :] = v
            return carry

        lax.fori_loop(0, 8, tile, 0)

    csk[0].wait_recv()
    add(r, x * 2 + 1 - k, True, False)
    for s in (1, 3, 2):
        csx[s].wait_recv()
        xq = (x + NX - s) % NX
        j = 2 * xq + k
        csk[s] = copy(st.at[j], st.at[j], s_sk.at[s], r_sk.at[s], at_k())
    for s in (1, 3, 2):
        csk[s].wait_recv()
        xq = (x + NX - s) % NX
        add(2 * xq + k, 2 * xq + 1 - k, False, s == 2)

    nb = BLK - IA
    v4 = im.reshape(NZ, NY, BLK, KC)
    cya, czb = {}, {}
    for s in (2, 1, 3):
        yq = (y + s) % NY
        sa[s] = v4[:, yq, :IA, :].astype(IDT)
        cya[s] = copy(sa.at[s], ya.at[s], s_ya.at[s], r_ya.at[s], at_y(s))
    for s in (4, 3, 5, 2, 6, 1, 7):
        zq = (z + s) % NZ
        sb[s] = v4[zq, :, IA:, :].astype(IDT)
        czb[s] = copy(sb.at[s], zb.at[s], s_zb.at[s], r_zb.at[s], at_z(s))
    ta[...] = v4[:, y, :IA, :]
    for s in (1, 3, 2):
        cya[s].wait_recv()
    ta[...] = (ta[...] + ya[1].astype(F32)) + (ya[2].astype(F32) + ya[3].astype(F32))
    cza = {}
    for s in (4, 3, 5, 2, 6, 1, 7):
        cza[s] = copy(ta.at[(z + s) % NZ], za.at[s], s_za.at[s], r_za.at[s], at_z(s))
    u = v4[z, :, IA:, :]
    for s in (1, 7, 2, 6, 3, 5, 4):
        czb[s].wait_recv()
        u = u + zb[s].astype(F32)
    ub[...] = u
    cyb = {}
    for s in (2, 1, 3):
        cyb[s] = copy(ub.at[(y + s) % NY], yb.at[s], s_yb.at[s], r_yb.at[s], at_y(s))
    low = ub[y]
    for s in (1, 3, 2):
        cyb[s].wait_recv()
        low = low + yb[s]
    high = ta[z]
    for s in (1, 7, 2, 6, 3, 5, 4):
        cza[s].wait_recv()
        high = high + za[s]
    scale = 65536.0**-0.5
    img_out[:IA, :] = high * scale
    img_out[IA:, :] = low * scale

    img = img_out[...]
    g0[...] = lax.dot_general(
        img, img, (((0,), (0,)), ((), ())),
        precision=lax.Precision.HIGHEST, preferred_element_type=F32,
    ) * (1.0 / 16384.0)
    half = pl.ds(pl.multiple_of(128 * k, 128), 128)
    other = pl.ds(pl.multiple_of(128 * (1 - k), 128), 128)
    cp = copy(g0.at[other], gk, s_q.at[0], r_q.at[0], at_k())
    cp.wait_recv()
    g1[...] = g0[half, :] + gk[...]
    cps = []
    for s in (2, 1, 3):
        piece = pl.ds(pl.multiple_of(32 * ((x + s) % NX), 32), 32)
        cps.append(copy(g1.at[piece], gx.at[s - 1], s_q.at[s], r_q.at[s], at_x(s)))
    for cp in cps:
        cp.wait_recv()
    g2[...] = (g1[pl.ds(pl.multiple_of(32 * x, 32), 32), :] + gx[0]) + (gx[1] + gx[2])
    cps = []
    for s in (2, 1, 3):
        piece = pl.ds(pl.multiple_of(8 * ((y + s) % NY), 8), 8)
        cps.append(copy(g2.at[piece], gy.at[s - 1], s_q.at[3 + s], r_q.at[3 + s], at_y(s)))
    for cp in cps:
        cp.wait_recv()
    gz[z] = (g2[pl.ds(pl.multiple_of(8 * y, 8), 8), :] + gy[0]) + (gy[1] + gy[2])
    cps = []
    for s in (4, 3, 5, 2, 6, 1, 7):
        cps.append(copy(gz.at[z], gz.at[z], s_q.at[6 + s], r_q.at[6 + s], at_z(s)))
    for cp in cps:
        cp.wait_recv()
    row8 = pl.ds(pl.multiple_of(128 * k + 32 * x + 8 * y, 8), 8)
    row32 = pl.ds(pl.multiple_of(128 * k + 32 * x, 32), 32)
    gf[row8, :] = ((gz[0] + gz[1]) + (gz[2] + gz[3])) + ((gz[4] + gz[5]) + (gz[6] + gz[7]))
    cps = []
    for s in (2, 1, 3):
        cps.append(copy(gf.at[row8], gf.at[row8], s_q.at[13 + s], r_q.at[13 + s], at_y(s)))
    for cp in cps:
        cp.wait_recv()
    cps = []
    for s in (2, 1, 3):
        cps.append(copy(gf.at[row32], gf.at[row32], s_q.at[16 + s], r_q.at[16 + s], at_x(s)))
    for cp in cps:
        cp.wait_recv()
    cp = copy(gf.at[half], gf.at[half], s_q.at[20], r_q.at[20], at_k())
    cp.wait_recv()
    gram_out[...] = gf[...]
    for cp in sends:
        cp.wait_send()


def image_and_gram(matrix, basis):
    dma = pltpu.SemaphoreType.DMA
    nb = BLK - IA
    sems = []
    for shape in (
        (NZ,), (NZ, NY), (NY,), (NZ,),
        (4,), (4,), (4,), (4,),
        (NY,), (NZ,), (NZ,), (NY,), (21,),
    ):
        sems += [dma(shape), dma(shape)]
    return pl.pallas_call(
        kernel,
        out_shape=(
            jax.ShapeDtypeStruct((BLK, KC), F32),
            jax.ShapeDtypeStruct((KC, KC), F32),
        ),
        in_specs=[pl.BlockSpec(memory_space=pl.ANY), pl.BlockSpec(memory_space=pltpu.VMEM)],
        out_specs=(pl.BlockSpec(memory_space=pltpu.VMEM), pl.BlockSpec(memory_space=pltpu.VMEM)),
        scratch_shapes=[
            pltpu.VMEM((8, 2048, 256), BF16),
            pltpu.VMEM((NZ, NY, BLK, KC), BF16),
            pltpu.VMEM((KC, 2048), BF16),
            pltpu.VMEM((4, KC, 256), F32),
            pltpu.VMEM((4, KC, 256), F32),
            pltpu.VMEM((KC, 256), F32),
            pltpu.VMEM((3, KC, 256), F32),
            pltpu.VMEM((3, KC, 256), F32),
            pltpu.VMEM((8, KC, 256), BF16),
            pltpu.VMEM((2048, KC), F32),
            pltpu.VMEM((NY, NZ, IA, KC), IDT),
            pltpu.VMEM((NZ, NY, nb, KC), IDT),
            pltpu.VMEM((NY, NZ, IA, KC), IDT),
            pltpu.VMEM((NZ, NY, nb, KC), IDT),
            pltpu.VMEM((NZ, IA, KC), F32),
            pltpu.VMEM((NY, nb, KC), F32),
            pltpu.VMEM((NZ, IA, KC), F32),
            pltpu.VMEM((NY, nb, KC), F32),
            pltpu.VMEM((KC, KC), F32),
            pltpu.VMEM((128, KC), F32),
            pltpu.VMEM((128, KC), F32),
            pltpu.VMEM((3, 32, KC), F32),
            pltpu.VMEM((32, KC), F32),
            pltpu.VMEM((3, 8, KC), F32),
            pltpu.VMEM((NZ, 8, KC), F32),
            pltpu.VMEM((KC, KC), F32),
            dma((8,)),
            *sems,
        ],
        compiler_params=pltpu.CompilerParams(
            collective_id=0, has_side_effects=True, vmem_limit_bytes=48 * 2**20
        ),
        cost_estimate=pl.CostEstimate(flops=2**33, bytes_accessed=2**23, transcendentals=0),
        name="image_and_gram",
    )(matrix, basis)


def body(matrix, basis):
    image, gram = image_and_gram(matrix, basis)
    lower = jnp.linalg.cholesky(gram)
    orthobasis = jax.scipy.linalg.solve_triangular(lower, image.T, lower=True).T
    return (orthobasis, lower.T)


def solution(mesh):
    in_specs = (P("row", "col"), P(("row", "col"), None))
    out_specs = (P(("row", "col"), None), P())
    return jax.shard_map(body, mesh=mesh, in_specs=in_specs, out_specs=out_specs, check_vma=False)
```

time: 716 us -> 166 us (0.23)
  waiting for transfers between devices: 619 us -> 0 us
  Pallas kernels: 0 us -> 102 us
  matrix products: 16.2 us -> 1.08 us
  between operations: 15.2 us -> 2.06 us
    psum x2 -> x0, waiting for transfers between devices: 328 us -> none  [the longest x1 257 us: body(): lower = jnp.linalg.cholesky(lax.psum(local_gram, ('row', 'col')))]
    unnamed x5 -> x0, waiting for transfers between devices: 213 us -> none
    pallas_call x0 -> x1, Pallas kernels: none -> 102 us  [image_and_gram(): pl.pallas_call(kernel, out_shape=(jax.ShapeDtypeStruct((BLK, KC), F32), j...]
    all_gather x1 -> x0, waiting for transfers between devices: 78.3 us -> none  [body(): lax.all_gather(basis, 'col', axis=0, tiled=True)]
    dot_general x3 -> x0, matrix products: 14.9 us -> none  [the longest x1 7.43 us: body(): lax.dot_general(matrix, lax.all_gather(basis, 'col', axis=0, tiled=True),...]
  transfers between devices with their start and end apart: 4 -> 0, of which waited for: 4 -> 0; matrix products, arithmetic and copies ran while one was open for 0% -> 0% of each run, Pallas kernels for 0% -> 0%
where the time goes in v1:
time: 166 us; the launch traced here: 165 us
  Pallas kernels  102 us (61%)
  other arithmetic  54.6 us (33%)
  local copies, waits for them, and re-layouts  5.87 us (4%)
  between operations  2.06 us (1%)
    pallas_call x1, Pallas kernels, image_and_gram(): pl.pallas_call(kernel, out_shape=(jax.ShapeDtypeStruct((BLK, KC), F32), j...  102 us
    another operation x6, other arithmetic, body(): lower = jnp.linalg.cholesky(gram)  34 us
    another operation x2, other arithmetic, body(): orthobasis = jax.scipy.linalg.solve_triangular(lower, image.T, lower=True).T  19.9 us
    another operation x6, local copies, waits for them, and re-layouts  4.06 us

profile of v1, /device:TPU:1, one launch (start us, length us, event | category | flops | bytes accessed | tf_op | source)
XLA Modules:
  0.0 165.3 jit_solution(1472826639311330907)
XLA Ops:
  0.6 0.0 copy-start
  0.6 0.7 copy-done
  1.4 101.7 %image_and_gram.1 = (f32[64,256]{1,0:T(8,128)S(1)}, f32[256,256]{1,0:T(8,128)S(1)}) custom-call(bf16[2048,2048]{1,0:T(8,128)(2,1)} %a_hbm.1, bf16[64,256]{1,0:T(8,128)(2,1)S(1)} %copy-done), custom_call_target="tpu_custom_call" | custom-call | flops 8589934592 | bytes 8388608 | tf_op jit(solution)/shard_map/image_and_gram/pallas_call | solution.py:252
  103.1 0.1 copy.4
  103.3 11.7 %cholesky.50 = f32[128,128]{1,0:T(8,128)S(1)} custom-call(f32[128,128]{1,0:T(8,128)S(1)} %cholesky.118), custom_call_target="Cholesky" | custom-call | tf_op jit(solution)/shard_map/jit(cholesky)/cholesky | solution.py:300
  115.1 9.8 %custom-call.15 = f32[1,128,128]{1,2,0:T(8,128)S(1)} custom-call(f32[1,128,128]{2,1,0:T(8,128)S(1)} %get-tuple-element.31), custom_call_target="InvertDiagBlocksLowerTriangular" | custom-call | tf_op jit(solution)/shard_map/jit(cholesky)/cholesky | solution.py:300
  124.9 0.2 constant_dynamic-update-slice_fusion.1
  125.1 0.3 convolution_subtract_fusion
  125.4 11.7 %cholesky.105 = f32[128,128]{1,0:T(8,128)S(1)} custom-call(f32[128,128]{1,0:T(8,128)S(1)} %convolution_subtract_fusion), custom_call_target="Cholesky" | custom-call | tf_op jit(solution)/shard_map/jit(cholesky)/cholesky | solution.py:300
  137.1 0.6 compare_reduce_fusion
  139.1 0.1 triangular_solve.57
  139.2 4.1 %while.1 = (s32[]{:T(128)}, f32[256,256]{1,0:T(8,128)S(1)}, s32[2,2]{1,0:T(2,128)S(1)}, f32[2,128,128]{2,1,0:T(8,128)S(1)}, s32[]{:T(128)}) while((s32[]{:T(128)}, f32[256,256]{1,0:T(8,128)S(1)}, s32[2,2]{1,0:T(2,128)S(1)}, f32[2,128,128]{2,1,0:T(8,128)S(1)}, s32[]{:T(128)}) %tuple.29), condition=%wide.while_cond, body=%wide.while_body.sunk | while | flops 2 | bytes 131181 | solution.py:301
  139.2 0.6 fusion.16
  139.8 1.4 bitcast_dynamic-update-slice_fusion.2
  141.3 0.6 fusion.16
  141.9 1.4 bitcast_dynamic-update-slice_fusion.2
  143.3 19.9 %custom-call.16 = f32[2,128,128]{1,2,0:T(8,128)S(1)} custom-call(f32[2,128,128]{2,1,0:T(8,128)S(1)} %get-tuple-element.13), custom_call_target="InvertDiagBlocksLowerTriangular" | custom-call | tf_op jit(solution)/shard_map/jit(_solve_triangular)/triangular_solve | solution.py:301
  163.2 0.2 fusion.5
  163.4 0.2 convolution_subtract_fusion.1
  163.7 0.2 fusion.4
  163.9 0.6 maximum_bitcast_fusion
  164.5 0.8 copy.5
  (10 shorter events, 0.2 us)
Async XLA Ops:
  0.6 0.8 copy-start

commit v2 on v1

--- a/solution.py
+++ b/solution.py
@@ -295,11 +295,75 @@
     )(matrix, basis)
 
 
+def factor(w, n):
+    w = list(w)
+    ng = len(w)
+    row = lax.broadcasted_iota(jnp.int32, (8, n), 0)
+    row1 = lax.broadcasted_iota(jnp.int32, (8, 128), 0)
+    out = []
+    for g in range(ng):
+        cur = w[g]
+        j0 = 8 * g
+        dc = [jnp.broadcast_to(cur[:, j0 + t : j0 + t + 1], (8, 128)) for t in range(8)]
+        z = cur
+        f = cur
+        for t in range(8):
+            d = jnp.broadcast_to(dc[t][t : t + 1, :], (8, 128))
+            rd = 1.0 / d
+            rs = lax.rsqrt(d)
+            rdn = jnp.concatenate([rd] * (n // 128), axis=1)
+            col = dc[t]
+            zrow = jnp.broadcast_to(z[t : t + 1, :], (8, n)) * rdn
+            coln = jnp.concatenate([col] * (n // 128), axis=1)
+            rsn = jnp.concatenate([rs] * (n // 128), axis=1)
+            f = jnp.where(row == t, f * rsn, jnp.where(row > t, z - coln * zrow, f))
+            z = jnp.where(row == t, zrow, z - coln * zrow)
+            for s in range(t + 1, 8):
+                e = jnp.broadcast_to(dc[s][t : t + 1, :], (8, 128)) * rd
+                dc[s] = jnp.where(row1 == t, e, dc[s] - col * e)
+        out.append(f)
+        for i in range(g + 1, ng):
+            acc = w[i]
+            for t in range(8):
+                cc = jnp.broadcast_to(w[i][:, j0 + t : j0 + t + 1], (8, n))
+                acc = acc - cc * jnp.broadcast_to(z[t : t + 1, :], (8, n))
+            w[i] = acc
+    return out
+
+def tail(gram, image, ortho, tri):
+    r8 = lax.broadcasted_iota(jnp.int32, (8, 128), 0)
+    c8 = lax.broadcasted_iota(jnp.int32, (8, 128), 1)
+    eye = [(r8 + 8 * g == c8).astype(F32) for g in range(16)]
+    w = [jnp.concatenate([gram[8 * g : 8 * g + 8, :], eye[g]], axis=1) for g in range(16)]
+    o = jnp.concatenate(factor(w, 384), axis=0)
+    rr = lax.broadcasted_iota(jnp.int32, (128, 128), 0)
+    cc = lax.broadcasted_iota(jnp.int32, (128, 128), 1)
+    up = cc >= rr
+    u11 = jnp.where(up, o[:, :128], 0.0)
+    u12 = o[:, 128:256]
+    i11 = o[:, 256:]
+    a22 = gram[128:, 128:] - lax.dot_general(u12, u12, (((0,), (0,)), ((), ())), precision=lax.Precision.HIGHEST, preferred_element_type=F32)
+    q1 = lax.dot_general(image[:, :128], i11, (((1,), (1,)), ((), ())), precision=lax.Precision.HIGHEST, preferred_element_type=F32)
+    rest = image[:, 128:] - jnp.dot(q1, u12, precision=lax.Precision.HIGHEST, preferred_element_type=F32)
+    w = [jnp.concatenate([a22[8 * g : 8 * g + 8, :], eye[g]], axis=1) for g in range(16)]
+    o2 = jnp.concatenate(factor(w, 256), axis=0)
+    q2 = lax.dot_general(rest, o2[:, 128:], (((1,), (1,)), ((), ())), precision=lax.Precision.HIGHEST, preferred_element_type=F32)
+    ortho[:, :128] = q1
+    ortho[:, 128:] = q2
+    tri[:128, :128] = u11
+    tri[:128, 128:] = u12
+    tri[128:, :128] = jnp.zeros((128, 128), F32)
+    tri[128:, 128:] = jnp.where(up, o2[:, :128], 0.0)
+
+def orthonormalise(image, gram):
+    v = pl.BlockSpec(memory_space=pltpu.VMEM)
+    return pl.pallas_call(tail,
+        out_shape=(jax.ShapeDtypeStruct(image.shape, F32), jax.ShapeDtypeStruct(gram.shape, F32)),
+        in_specs=[v, v], out_specs=(v, v), name="orthonormalise")(gram, image)
+
+
 def body(matrix, basis):
-    image, gram = image_and_gram(matrix, basis)
-    lower = jnp.linalg.cholesky(gram)
-    orthobasis = jax.scipy.linalg.solve_triangular(lower, image.T, lower=True).T
-    return (orthobasis, lower.T)
+    return orthonormalise(*image_and_gram(matrix, basis))
 
 
 def solution(mesh):

time: 166 us -> 116 us (0.70)
  other arithmetic: 54.6 us -> 0 us
  Pallas kernels: 102 us -> 113 us
  local copies, waits for them, and re-layouts: 5.87 us -> 2.06 us
    another operation x8 -> x0, other arithmetic: 53.9 us -> none  [the longest x6 34 us: body(): lower = jnp.linalg.cholesky(gram)]
    pallas_call x0 -> x1, Pallas kernels: none -> 11.4 us  [orthonormalise(): pl.pallas_call(tail, out_shape=(jax.ShapeDtypeStruct(image.shape, F32), j...]
    another operation x9 -> x0, local copies, waits for them, and re-layouts: 4.16 us -> none
where the time goes in v2:
time: 116 us
  Pallas kernels  113 us (97%)
  local copies, waits for them, and re-layouts  2.06 us (2%)
    pallas_call x1, Pallas kernels, image_and_gram(): pl.pallas_call(kernel, out_shape=(jax.ShapeDtypeStruct((BLK, KC), F32), j...  102 us
    pallas_call x1, Pallas kernels, orthonormalise(): pl.pallas_call(tail, out_shape=(jax.ShapeDtypeStruct(image.shape, F32), j...  11.4 us

profile of v2, /device:TPU:1, one launch (start us, length us, event | category | flops | bytes accessed | tf_op | source)
XLA Modules:
  0.0 115.9 jit_solution(10686624954026022082)
XLA Ops:
  0.6 0.0 copy-start.2
  0.6 0.7 copy-done.2
  1.4 101.7 %image_and_gram.1 = (f32[64,256]{1,0:T(8,128)S(1)}, f32[256,256]{1,0:T(8,128)S(1)}) custom-call(bf16[2048,2048]{1,0:T(8,128)(2,1)} %a_hbm.1, bf16[64,256]{1,0:T(8,128)(2,1)S(1)} %copy-done.2), custom_call_target="tpu_custom_call" | custom-call | flops 8589934592 | bytes 8388608 | tf_op jit(solution)/shard_map/image_and_gram/pallas_call | solution.py:252
  103.1 0.0 copy-start
  103.1 0.7 copy-done
  103.8 0.0 copy-start.1
  103.8 0.6 copy-done.1
  104.4 11.4 %orthonormalise.1 = (f32[64,256]{1,0:T(8,128)}, f32[256,256]{1,0:T(8,128)}) custom-call(f32[256,256]{1,0:T(8,128)} %copy-done, f32[64,256]{1,0:T(8,128)} %copy-done.1), custom_call_target="tpu_custom_call" | custom-call | tf_op jit(solution)/shard_map/orthonormalise/pallas_call | solution.py:360
Async XLA Ops:
  0.6 0.8 copy-start.2
  103.1 0.7 copy-start
  103.8 0.6 copy-start.1

commit v3 on v2

v3 whole, which is shorter than its diff:
```python
import jax
import jax.numpy as jnp
from jax import lax
from jax.experimental import pallas as pl
from jax.experimental.pallas import tpu as pltpu
from jax.sharding import PartitionSpec as P

F32 = jnp.float32
BF16 = jnp.bfloat16
NX, NY, NZ = 4, 4, 8
KC = 256
BLK = 64
GA = 48
IA = 48
IDT = BF16
XS = (2, 1, 3, 0)


def kernel(
    a_hbm, basis, img_out, gram_out,
    av, g, bt, part, rk, own, xs, xr, st, im, sa, sb, ya, zb, ta, ub, za, yb,
    g0, gk, g1, gx, gz, gf,
    asem, s_gz, r_gz, s_gzy, r_gzy, s_gy, r_gy, s_gyz, r_gyz,
    s_k, r_k, s_x, r_x, s_sx, r_sx, s_sk, r_sk,
    s_ya, r_ya, s_zb, r_zb, s_za, r_za, s_yb, r_yb,
    s_q, r_q,
):
    r = lax.axis_index("row")
    c = lax.axis_index("col")
    x, k = r // 2, r % 2
    z, y = c // NY, c % NY

    def at_xy(s, t):
        return (((x + s) % NX) * 2 + k, z * NY + (y + t) % NY)

    def at_x(s):
        return at_xy(s, 0)

    def at_k():
        return (x * 2 + 1 - k, c)

    def at_y(s):
        return at_xy(0, s)

    def at_z(s):
        return (r, ((z + s) % NZ) * NY + y)

    shifts = [(s, t) for s in range(NX) for t in range(NY) if s or t]
    far = (4, 3, 5, 2, 6, 1, 7)
    near = (1, 7, 2, 6, 3, 5, 4)
    halves = range(2)

    loads = []
    for j in range(8):
        cp = pltpu.make_async_copy(a_hbm.at[:, pl.ds(256 * j, 256)], av.at[j], asem.at[j])
        cp.start()
        loads.append(cp)

    barrier = pltpu.get_barrier_semaphore()
    for s in far:
        pl.semaphore_signal(barrier, 1, device_id=at_z(s))
    for s, t in shifts:
        pl.semaphore_signal(barrier, 1, device_id=at_xy(s, t))
    pl.semaphore_signal(barrier, 1, device_id=at_k())
    for h in halves:
        g[h, z, y] = basis[:, 128 * h : 128 * h + 128]
    pl.semaphore_wait(barrier, NZ - 1 + NX * NY - 1 + 1)

    sends = []

    def copy(src, dst, ss, rs, dev):
        cp = pltpu.make_async_remote_copy(src, dst, ss, rs, device_id=dev)
        cp.start()
        sends.append(cp)
        return cp

    hi, lo = pl.ds(0, GA), pl.ds(GA, BLK - GA)
    cy, cz, cyz, czy = {}, {}, {}, {}
    for h in halves:
        k128 = pl.ds(128 * h, 128)
        for s in near:
            cz[h, s] = copy(basis.at[hi, k128], g.at[h, z, y, hi], s_gz.at[h, s], r_gz.at[h, s], at_z(s))
        for s in (2, 1, 3):
            cy[h, s] = copy(basis.at[lo, k128], g.at[h, z, y, lo], s_gy.at[h, s], r_gy.at[h, s], at_y(s))
        for t in (2, 1, 3):
            czy[h, 0, t] = copy(basis.at[hi, k128], g.at[h, z, y, hi], s_gzy.at[h, 0, t], r_gzy.at[h, 0, t], at_y(t))
    for h in halves:
        for s in (1, 3, 2):
            cy[h, s].wait_recv()
        for s in far:
            cyz[h, s] = copy(g.at[h, z, :, lo], g.at[h, z, :, lo], s_gyz.at[h, s], r_gyz.at[h, s], at_z(s))
        for s in near:
            cz[h, s].wait_recv()
            zs = (z + NZ - s) % NZ
            for t in (2, 1, 3):
                czy[h, s, t] = copy(
                    g.at[h, zs, y, hi], g.at[h, zs, y, hi], s_gzy.at[h, s, t], r_gzy.at[h, s, t], at_y(t)
                )

    def product(h, j):
        return jnp.dot(bt[h], av[j], preferred_element_type=F32)

    cx = {}
    for h in halves:
        for s in far:
            cyz[h, s].wait_recv()
        for s in (0, *near):
            for t in (1, 3, 2):
                czy[h, s, t].wait_recv()

        def turn(i, carry):
            bt[h, :, pl.ds(pl.multiple_of(i * 256, 256), 256)] = g[h, i].reshape(NY * BLK, 128).T
            return carry

        lax.fori_loop(0, NZ, turn, 0)
        if h == 0:
            for cp in loads:
                cp.wait()
        ck = []
        for i, s in enumerate(XS):
            part[h, i] = product(h, 2 * ((x + s) % NX) + 1 - k)
            ck.append(copy(part.at[h, i], rk.at[h, i], s_k.at[h, i], r_k.at[h, i], at_k()))
        for i, s in enumerate(XS):
            p = product(h, 2 * ((x + s) % NX) + k)
            ck[i].wait_recv()
            p = p + rk[h, i]
            if s:
                xs[h, i] = p
                cx[h, i] = copy(xs.at[h, i], xr.at[h, i], s_x.at[h, i], r_x.at[h, i], at_x(s))
            else:
                own[h] = p
    csx, csk = {}, {}
    for h in halves:
        for i in (1, 2, 0):
            cx[h, i].wait_recv()
        total = (own[h] + xr[h, 0]) + (xr[h, 1] + xr[h, 2])
        st[h, r] = (total * (16384.0**-0.5)).astype(BF16)
        mine = st.at[h, r]
        for s in (2, 1, 3):
            csx[h, s] = copy(mine, mine, s_sx.at[h, s], r_sx.at[h, s], at_x(s))
        csk[h, 0] = copy(mine, mine, s_sk.at[h, 0], r_sk.at[h, 0], at_k())

    nb = BLK - IA
    cya, czb, cza, cyb = {}, {}, {}, {}
    for h in halves:

        def add(ja, jb, first):
            def tile(i, carry):
                rows = pl.ds(pl.multiple_of(i * 256, 256), 256)
                dims = (((1,), (1,)), ((), ()))
                v = lax.dot_general(av[ja, rows, :], st[h, ja], dims, preferred_element_type=F32)
                v += lax.dot_general(av[jb, rows, :], st[h, jb], dims, preferred_element_type=F32)
                if not first:
                    v += im[h, rows, :]
                im[h, rows, :] = v
                return carry

            lax.fori_loop(0, 8, tile, 0)

        csk[h, 0].wait_recv()
        add(r, x * 2 + 1 - k, True)
        for s in (1, 3, 2):
            csx[h, s].wait_recv()
            j = 2 * ((x + NX - s) % NX) + k
            csk[h, s] = copy(st.at[h, j], st.at[h, j], s_sk.at[h, s], r_sk.at[h, s], at_k())
        for s in (1, 3, 2):
            csk[h, s].wait_recv()
            xq = (x + NX - s) % NX
            add(2 * xq + k, 2 * xq + 1 - k, False)
        v4 = im.reshape(2, NZ, NY, BLK, 128)
        for s in (2, 1, 3):
            sa[h, s] = v4[h, :, (y + s) % NY, :IA, :].astype(IDT)
            cya[h, s] = copy(sa.at[h, s], ya.at[h, s], s_ya.at[h, s], r_ya.at[h, s], at_y(s))
        for s in far:
            sb[h, s] = v4[h, (z + s) % NZ, :, IA:, :].astype(IDT)
            czb[h, s] = copy(sb.at[h, s], zb.at[h, s], s_zb.at[h, s], r_zb.at[h, s], at_z(s))
        ta[h] = v4[h, :, y, :IA, :]
        ub[h] = v4[h, z, :, IA:, :]
    for h in halves:
        for s in (1, 3, 2):
            cya[h, s].wait_recv()
        ta[h] = (ta[h] + ya[h, 1].astype(F32)) + (ya[h, 2].astype(F32) + ya[h, 3].astype(F32))
        for s in far:
            cza[h, s] = copy(ta.at[h, (z + s) % NZ], za.at[h, s], s_za.at[h, s], r_za.at[h, s], at_z(s))
        u = ub[h]
        for s in near:
            czb[h, s].wait_recv()
            u = u + zb[h, s].astype(F32)
        ub[h] = u
        for s in (2, 1, 3):
            cyb[h, s] = copy(ub.at[h, (y + s) % NY], yb.at[h, s], s_yb.at[h, s], r_yb.at[h, s], at_y(s))
    scale = 65536.0**-0.5
    for h in halves:
        low = ub[h, y]
        for s in (1, 3, 2):
            cyb[h, s].wait_recv()
            low = low + yb[h, s]
        high = ta[h, z]
        for s in near:
            cza[h, s].wait_recv()
            high = high + za[h, s]
        img_out[:IA, 128 * h : 128 * h + 128] = high * scale
        img_out[IA:, 128 * h : 128 * h + 128] = low * scale

    img = img_out[...]
    g0[...] = lax.dot_general(
        img, img, (((0,), (0,)), ((), ())),
        precision=lax.Precision.HIGHEST, preferred_element_type=F32,
    ) * (1.0 / 16384.0)
    half = pl.multiple_of(128 * k, 128)
    cp = copy(g0.at[pl.ds(pl.multiple_of(128 * (1 - k), 128), 128)], gk, s_q.at[0], r_q.at[0], at_k())
    cp.wait_recv()
    g1[...] = g0[pl.ds(half, 128), :] + gk[...]

    def rows8(xq, yq):
        return pl.ds(pl.multiple_of(32 * xq + 8 * yq, 8), 8)

    cps = []
    for s, t in sorted(shifts, key=lambda v: -min(v[0], NX - v[0]) - min(v[1], NY - v[1])):
        q = NY * s + t
        piece = g1.at[rows8((x + s) % NX, (y + t) % NY)]
        cps.append(copy(piece, gx.at[q], s_q.at[q], r_q.at[q], at_xy(s, t)))
    acc = g1[rows8(x, y), :]
    for (s, t), cp in zip(reversed(shifts), reversed(cps)):
        cp.wait_recv()
    for s, t in shifts:
        acc = acc + gx[NY * s + t]
    gz[z] = acc
    cps = []
    for s in far:
        cps.append(copy(gz.at[z], gz.at[z], s_q.at[15 + s], r_q.at[15 + s], at_z(s)))
    for cp in cps:
        cp.wait_recv()
    row8 = pl.ds(pl.multiple_of(half + 32 * x + 8 * y, 8), 8)
    gf[row8, :] = ((gz[0] + gz[1]) + (gz[2] + gz[3])) + ((gz[4] + gz[5]) + (gz[6] + gz[7]))
    cps = {}
    for s, t in sorted(shifts, key=lambda v: -min(v[0], NX - v[0]) - min(v[1], NY - v[1])):
        q = 23 + NY * s + t
        cps[s, t] = copy(gf.at[row8], gf.at[row8], s_q.at[q], r_q.at[q], at_xy(s, t))
    ckf = []
    for s in (0, 1, 3, 2):
        for t in range(NY):
            if s or t:
                cps[s, t].wait_recv()
        row32 = gf.at[pl.ds(pl.multiple_of(half + 32 * ((x + NX - s) % NX), 32), 32)]
        ckf.append(copy(row32, row32, s_q.at[39 + s], r_q.at[39 + s], at_k()))
    for cp in ckf:
        cp.wait_recv()
    gram_out[...] = gf[...]
    for cp in sends:
        cp.wait_send()


def image_and_gram(matrix, basis):
    dma = pltpu.SemaphoreType.DMA
    nb = BLK - IA
    sems = []
    for shape in (
        (2, NZ), (2, NZ, NY), (2, NY), (2, NZ),
        (2, 4), (2, 3), (2, 4), (2, 4),
        (2, NY), (2, NZ), (2, NZ), (2, NY), (43,),
    ):
        sems += [dma(shape), dma(shape)]
    return pl.pallas_call(
        kernel,
        out_shape=(
            jax.ShapeDtypeStruct((BLK, KC), F32),
            jax.ShapeDtypeStruct((KC, KC), F32),
        ),
        in_specs=[pl.BlockSpec(memory_space=pl.ANY), pl.BlockSpec(memory_space=pltpu.VMEM)],
        out_specs=(pl.BlockSpec(memory_space=pltpu.VMEM), pl.BlockSpec(memory_space=pltpu.VMEM)),
        scratch_shapes=[
            pltpu.VMEM((8, 2048, 256), BF16),
            pltpu.VMEM((2, NZ, NY, BLK, 128), BF16),
            pltpu.VMEM((2, 128, 2048), BF16),
            pltpu.VMEM((2, 4, 128, 256), F32),
            pltpu.VMEM((2, 4, 128, 256), F32),
            pltpu.VMEM((2, 128, 256), F32),
            pltpu.VMEM((2, 3, 128, 256), F32),
            pltpu.VMEM((2, 3, 128, 256), F32),
            pltpu.VMEM((2, 8, 128, 256), BF16),
            pltpu.VMEM((2, 2048, 128), F32),
            pltpu.VMEM((2, NY, NZ, IA, 128), IDT),
            pltpu.VMEM((2, NZ, NY, nb, 128), IDT),
            pltpu.VMEM((2, NY, NZ, IA, 128), IDT),
            pltpu.VMEM((2, NZ, NY, nb, 128), IDT),
            pltpu.VMEM((2, NZ, IA, 128), F32),
            pltpu.VMEM((2, NY, nb, 128), F32),
            pltpu.VMEM((2, NZ, IA, 128), F32),
            pltpu.VMEM((2, NY, nb, 128), F32),
            pltpu.VMEM((KC, KC), F32),
            pltpu.VMEM((128, KC), F32),
            pltpu.VMEM((128, KC), F32),
            pltpu.VMEM((NX * NY, 8, KC), F32),
            pltpu.VMEM((NZ, 8, KC), F32),
            pltpu.VMEM((KC, KC), F32),
            dma((8,)),
            *sems,
        ],
        compiler_params=pltpu.CompilerParams(
            collective_id=0, has_side_effects=True, vmem_limit_bytes=48 * 2**20
        ),
        cost_estimate=pl.CostEstimate(flops=2**33, bytes_accessed=2**23, transcendentals=0),
        name="image_and_gram",
    )(matrix, basis)


def factor(w, n):
    w = list(w)
    ng = len(w)
    row = lax.broadcasted_iota(jnp.int32, (8, n), 0)
    row1 = lax.broadcasted_iota(jnp.int32, (8, 128), 0)
    out = []
    for g in range(ng):
        cur = w[g]
        j0 = 8 * g
        dc = [jnp.broadcast_to(cur[:, j0 + t : j0 + t + 1], (8, 128)) for t in range(8)]
        z = cur
        f = cur
        for t in range(8):
            d = jnp.broadcast_to(dc[t][t : t + 1, :], (8, 128))
            rd = 1.0 / d
            rs = lax.rsqrt(d)
            rdn = jnp.concatenate([rd] * (n // 128), axis=1)
            col = dc[t]
            zrow = jnp.broadcast_to(z[t : t + 1, :], (8, n)) * rdn
            coln = jnp.concatenate([col] * (n // 128), axis=1)
            rsn = jnp.concatenate([rs] * (n // 128), axis=1)
            f = jnp.where(row == t, f * rsn, jnp.where(row > t, z - coln * zrow, f))
            z = jnp.where(row == t, zrow, z - coln * zrow)
            for s in range(t + 1, 8):
                e = jnp.broadcast_to(dc[s][t : t + 1, :], (8, 128)) * rd
                dc[s] = jnp.where(row1 == t, e, dc[s] - col * e)
        out.append(f)
        for i in range(g + 1, ng):
            acc = w[i]
            for t in range(8):
                cc = jnp.broadcast_to(w[i][:, j0 + t : j0 + t + 1], (8, n))
                acc = acc - cc * jnp.broadcast_to(z[t : t + 1, :], (8, n))
            w[i] = acc
    return out

def tail(gram, image, ortho, tri):
    r8 = lax.broadcasted_iota(jnp.int32, (8, 128), 0)
    c8 = lax.broadcasted_iota(jnp.int32, (8, 128), 1)
    eye = [(r8 + 8 * g == c8).astype(F32) for g in range(16)]
    w = [jnp.concatenate([gram[8 * g : 8 * g + 8, :], eye[g]], axis=1) for g in range(16)]
    o = jnp.concatenate(factor(w, 384), axis=0)
    rr = lax.broadcasted_iota(jnp.int32, (128, 128), 0)
    cc = lax.broadcasted_iota(jnp.int32, (128, 128), 1)
    up = cc >= rr
    u11 = jnp.where(up, o[:, :128], 0.0)
    u12 = o[:, 128:256]
    i11 = o[:, 256:]
    a22 = gram[128:, 128:] - lax.dot_general(u12, u12, (((0,), (0,)), ((), ())), precision=lax.Precision.HIGHEST, preferred_element_type=F32)
    q1 = lax.dot_general(image[:, :128], i11, (((1,), (1,)), ((), ())), precision=lax.Precision.HIGHEST, preferred_element_type=F32)
    rest = image[:, 128:] - jnp.dot(q1, u12, precision=lax.Precision.HIGHEST, preferred_element_type=F32)
    w = [jnp.concatenate([a22[8 * g : 8 * g + 8, :], eye[g]], axis=1) for g in range(16)]
    o2 = jnp.concatenate(factor(w, 256), axis=0)
    q2 = lax.dot_general(rest, o2[:, 128:], (((1,), (1,)), ((), ())), precision=lax.Precision.HIGHEST, preferred_element_type=F32)
    ortho[:, :128] = q1
    ortho[:, 128:] = q2
    tri[:128, :128] = u11
    tri[:128, 128:] = u12
    tri[128:, :128] = jnp.zeros((128, 128), F32)
    tri[128:, 128:] = jnp.where(up, o2[:, :128], 0.0)

def orthonormalise(image, gram):
    v = pl.BlockSpec(memory_space=pltpu.VMEM)
    return pl.pallas_call(tail,
        out_shape=(jax.ShapeDtypeStruct(image.shape, F32), jax.ShapeDtypeStruct(gram.shape, F32)),
        in_specs=[v, v], out_specs=(v, v), name="orthonormalise")(gram, image)


def body(matrix, basis):
    return orthonormalise(*image_and_gram(matrix, basis))


def solution(mesh):
    in_specs = (P("row", "col"), P(("row", "col"), None))
    out_specs = (P(("row", "col"), None), P())
    return jax.shard_map(body, mesh=mesh, in_specs=in_specs, out_specs=out_specs, check_vma=False)
```

time: 116 us -> 105 us (0.905)
  Pallas kernels: 113 us -> 102 us
    pallas_call x1, Pallas kernels: 102 us -> 90.5 us  [image_and_gram(): pl.pallas_call(kernel, out_shape=(jax.ShapeDtypeStruct((BLK, KC), F32), j...]
where the time goes in v3:
time: 105 us
  Pallas kernels  102 us (97%)
  local copies, waits for them, and re-layouts  2.06 us (2%)
    pallas_call x1, Pallas kernels, image_and_gram(): pl.pallas_call(kernel, out_shape=(jax.ShapeDtypeStruct((BLK, KC), F32), j...  90.5 us
    pallas_call x1, Pallas kernels, orthonormalise(): pl.pallas_call(tail, out_shape=(jax.ShapeDtypeStruct(image.shape, F32), j...  11.4 us

profile of v3, /device:TPU:1, one launch (start us, length us, event | category | flops | bytes accessed | tf_op | source)
XLA Modules:
  0.0 104.6 jit_solution(15662357441399433523)
XLA Ops:
  0.6 0.0 copy-start.2
  0.6 0.7 copy-done.2
  1.4 90.5 %image_and_gram.1 = (f32[64,256]{1,0:T(8,128)S(1)}, f32[256,256]{1,0:T(8,128)S(1)}) custom-call(bf16[2048,2048]{1,0:T(8,128)(2,1)} %a_hbm.1, bf16[64,256]{1,0:T(8,128)(2,1)S(1)} %copy-done.2), custom_call_target="tpu_custom_call" | custom-call | flops 8589934592 | bytes 8388608 | tf_op jit(solution)/shard_map/image_and_gram/pallas_call | solution.py:264
  91.9 0.0 copy-start
  91.9 0.7 copy-done
  92.6 0.0 copy-start.1
  92.6 0.6 copy-done.1
  93.2 11.4 %orthonormalise.1 = (f32[64,256]{1,0:T(8,128)}, f32[256,256]{1,0:T(8,128)}) custom-call(f32[256,256]{1,0:T(8,128)} %copy-done, f32[64,256]{1,0:T(8,128)} %copy-done.1), custom_call_target="tpu_custom_call" | custom-call | tf_op jit(solution)/shard_map/orthonormalise/pallas_call | solution.py:370
Async XLA Ops:
  0.6 0.8 copy-start.2
  91.9 0.7 copy-start
  92.6 0.6 copy-start.1

commit v4 on v3

--- a/solution.py
+++ b/solution.py
@@ -17,8 +17,8 @@
 
 
 def kernel(
-    a_hbm, basis, img_out, gram_out,
-    av, g, bt, part, rk, own, xs, xr, st, im, sa, sb, ya, zb, ta, ub, za, yb,
+    a_hbm, b_hbm, img_out, gram_out,
+    av, basis, g, bt, part, rk, own, xs, xr, st, im, sa, sb, ya, zb, ta, ub, za, yb,
     g0, gk, g1, gx, gz, gf,
     asem, s_gz, r_gz, s_gzy, r_gzy, s_gy, r_gy, s_gyz, r_gyz,
     s_k, r_k, s_x, r_x, s_sx, r_sx, s_sk, r_sk,
@@ -50,6 +50,8 @@
     near = (1, 7, 2, 6, 3, 5, 4)
     halves = range(2)
 
+    first = pltpu.make_async_copy(b_hbm, basis, asem.at[8])
+    first.start()
     loads = []
     for j in range(8):
         cp = pltpu.make_async_copy(a_hbm.at[:, pl.ds(256 * j, 256)], av.at[j], asem.at[j])
@@ -59,12 +61,15 @@
     barrier = pltpu.get_barrier_semaphore()
     for s in far:
         pl.semaphore_signal(barrier, 1, device_id=at_z(s))
-    for s, t in shifts:
-        pl.semaphore_signal(barrier, 1, device_id=at_xy(s, t))
+    for s in range(1, NY):
+        pl.semaphore_signal(barrier, 1, device_id=at_y(s))
+    for s in range(1, NX):
+        pl.semaphore_signal(barrier, 1, device_id=at_x(s))
     pl.semaphore_signal(barrier, 1, device_id=at_k())
+    first.wait()
     for h in halves:
         g[h, z, y] = basis[:, 128 * h : 128 * h + 128]
-    pl.semaphore_wait(barrier, NZ - 1 + NX * NY - 1 + 1)
+    pl.semaphore_wait(barrier, NZ + NY + NX - 3 + 1)
 
     sends = []
 
@@ -108,11 +113,8 @@
             for t in (1, 3, 2):
                 czy[h, s, t].wait_recv()
 
-        def turn(i, carry):
-            bt[h, :, pl.ds(pl.multiple_of(i * 256, 256), 256)] = g[h, i].reshape(NY * BLK, 128).T
-            return carry
-
-        lax.fori_loop(0, NZ, turn, 0)
+        for i in range(NZ):
+            bt[h, :, 256 * i : 256 * i + 256] = g[h, i].reshape(NY * BLK, 128).T
         if h == 0:
             for cp in loads:
                 cp.wait()
@@ -145,17 +147,14 @@
     for h in halves:
 
         def add(ja, jb, first):
-            def tile(i, carry):
-                rows = pl.ds(pl.multiple_of(i * 256, 256), 256)
-                dims = (((1,), (1,)), ((), ()))
+            dims = (((1,), (1,)), ((), ()))
+            for i in range(8):
+                rows = pl.ds(256 * i, 256)
                 v = lax.dot_general(av[ja, rows, :], st[h, ja], dims, preferred_element_type=F32)
                 v += lax.dot_general(av[jb, rows, :], st[h, jb], dims, preferred_element_type=F32)
                 if not first:
                     v += im[h, rows, :]
                 im[h, rows, :] = v
-                return carry
-
-            lax.fori_loop(0, 8, tile, 0)
 
         csk[h, 0].wait_recv()
         add(r, x * 2 + 1 - k, True)
@@ -267,10 +266,11 @@
             jax.ShapeDtypeStruct((BLK, KC), F32),
             jax.ShapeDtypeStruct((KC, KC), F32),
         ),
-        in_specs=[pl.BlockSpec(memory_space=pl.ANY), pl.BlockSpec(memory_space=pltpu.VMEM)],
+        in_specs=[pl.BlockSpec(memory_space=pltpu.HBM)] * 2,
         out_specs=(pl.BlockSpec(memory_space=pltpu.VMEM), pl.BlockSpec(memory_space=pltpu.VMEM)),
         scratch_shapes=[
             pltpu.VMEM((8, 2048, 256), BF16),
+            pltpu.VMEM((BLK, KC), BF16),
             pltpu.VMEM((2, NZ, NY, BLK, 128), BF16),
             pltpu.VMEM((2, 128, 2048), BF16),
             pltpu.VMEM((2, 4, 128, 256), F32),
@@ -294,7 +294,7 @@
             pltpu.VMEM((NX * NY, 8, KC), F32),
             pltpu.VMEM((NZ, 8, KC), F32),
             pltpu.VMEM((KC, KC), F32),
-            dma((8,)),
+            dma((9,)),
             *sems,
         ],
         compiler_params=pltpu.CompilerParams(
@@ -369,7 +369,8 @@
     v = pl.BlockSpec(memory_space=pltpu.VMEM)
     return pl.pallas_call(tail,
         out_shape=(jax.ShapeDtypeStruct(image.shape, F32), jax.ShapeDtypeStruct(gram.shape, F32)),
-        in_specs=[v, v], out_specs=(v, v), name="orthonormalise")(gram, image)
+        in_specs=[v, v], out_specs=(v, v), name="orthonormalise",
+        compiler_params=pltpu.CompilerParams(vmem_limit_bytes=16 * 2**20))(gram, image)
 
 
 def body(matrix, basis):

time: 105 us -> 94.8 us (0.903)
  Pallas kernels: 102 us -> 93.2 us
  local copies, waits for them, and re-layouts: 2.06 us -> 0.75 us
    pallas_call x1, Pallas kernels: 90.5 us -> 82.6 us  [image_and_gram(): pl.pallas_call(kernel, out_shape=(jax.ShapeDtypeStruct((BLK, KC), F32), j...]
    unnamed x6 -> x2, local copies, waits for them, and re-layouts: 2.06 us -> 0.75 us
where the time goes in v4:
time: 94.8 us; the launch traced here: 94.6 us
  Pallas kernels  93.2 us (98%)
    pallas_call x1, Pallas kernels, image_and_gram(): pl.pallas_call(kernel, out_shape=(jax.ShapeDtypeStruct((BLK, KC), F32), j...  82.6 us
    pallas_call x1, Pallas kernels, orthonormalise(): pl.pallas_call(tail, out_shape=(jax.ShapeDtypeStruct(image.shape, F32), j...  10.7 us

profile of v4, /device:TPU:1, one launch (start us, length us, event | category | flops | bytes accessed | tf_op | source)
XLA Modules:
  0.0 94.6 jit_solution(327055083155634710)
XLA Ops:
  0.6 0.0 copy-start
  0.6 0.7 copy-done
  1.4 82.6 %image_and_gram.1 = (f32[64,256]{1,0:T(8,128)S(1)}, f32[256,256]{1,0:T(8,128)S(1)}) custom-call(bf16[2048,2048]{1,0:T(8,128)(2,1)} %a_hbm.1, bf16[64,256]{1,0:T(8,128)(2,1)S(1)} %copy-done), custom_call_target="tpu_custom_call" | custom-call | flops 8589934592 | bytes 8388608 | tf_op jit(solution)/shard_map/image_and_gram/pallas_call | solution.py:263
  83.9 10.7 %orthonormalise.1 = (f32[64,256]{1,0:T(8,128)}, f32[256,256]{1,0:T(8,128)}) custom-call(f32[256,256]{1,0:T(8,128)S(1)} %get-tuple-element.4.gram, f32[64,256]{1,0:T(8,128)S(1)} %get-tuple-element.5.image), custom_call_target="tpu_custom_call" | custom-call | tf_op jit(solution)/shard_map/orthonormalise/pallas_call | solution.py:370
Async XLA Ops:
  0.6 0.8 copy-start

commit v5 on v4

--- a/solution.py
+++ b/solution.py
@@ -14,11 +14,12 @@
 IA = 48
 IDT = BF16
 XS = (2, 1, 3, 0)
+XFAR, XNEAR = BF16, F32
 
 
 def kernel(
     a_hbm, b_hbm, img_out, gram_out,
-    av, basis, g, bt, part, rk, own, xs, xr, st, im, sa, sb, ya, zb, ta, ub, za, yb,
+    av, basis, g, bt, part, rk, own, xs2, xs1, xr2, xr1, st, im, sa, sb, ya, zb, ta, ub, za, yb,
     g0, gk, g1, gx, gz, gf,
     asem, s_gz, r_gz, s_gzy, r_gzy, s_gy, r_gy, s_gyz, r_gyz,
     s_k, r_k, s_x, r_x, s_sx, r_sx, s_sk, r_sk,
@@ -127,15 +128,16 @@
             ck[i].wait_recv()
             p = p + rk[h, i]
             if s:
-                xs[h, i] = p
-                cx[h, i] = copy(xs.at[h, i], xr.at[h, i], s_x.at[h, i], r_x.at[h, i], at_x(s))
+                src, dst = (xs2.at[h], xr2.at[h]) if s == 2 else (xs1.at[h, i - 1], xr1.at[h, i - 1])
+                src[...] = p.astype(src.dtype)
+                cx[h, i] = copy(src, dst, s_x.at[h, i], r_x.at[h, i], at_x(s))
             else:
                 own[h] = p
     csx, csk = {}, {}
     for h in halves:
         for i in (1, 2, 0):
             cx[h, i].wait_recv()
-        total = (own[h] + xr[h, 0]) + (xr[h, 1] + xr[h, 2])
+        total = (own[h] + xr2[h].astype(F32)) + (xr1[h, 0].astype(F32) + xr1[h, 1].astype(F32))
         st[h, r] = (total * (16384.0**-0.5)).astype(BF16)
         mine = st.at[h, r]
         for s in (2, 1, 3):
@@ -276,8 +278,10 @@
             pltpu.VMEM((2, 4, 128, 256), F32),
             pltpu.VMEM((2, 4, 128, 256), F32),
             pltpu.VMEM((2, 128, 256), F32),
-            pltpu.VMEM((2, 3, 128, 256), F32),
-            pltpu.VMEM((2, 3, 128, 256), F32),
+            pltpu.VMEM((2, 128, 256), XFAR),
+            pltpu.VMEM((2, 2, 128, 256), XNEAR),
+            pltpu.VMEM((2, 128, 256), XFAR),
+            pltpu.VMEM((2, 2, 128, 256), XNEAR),
             pltpu.VMEM((2, 8, 128, 256), BF16),
             pltpu.VMEM((2, 2048, 128), F32),
             pltpu.VMEM((2, NY, NZ, IA, 128), IDT),
@@ -310,27 +314,38 @@
     ng = len(w)
     row = lax.broadcasted_iota(jnp.int32, (8, n), 0)
     row1 = lax.broadcasted_iota(jnp.int32, (8, 128), 0)
+    wide = lambda v: jnp.concatenate([v] * (n // 128), axis=1)
     out = []
     for g in range(ng):
-        cur = w[g]
+        z = f = w[g]
         j0 = 8 * g
-        dc = [jnp.broadcast_to(cur[:, j0 + t : j0 + t + 1], (8, 128)) for t in range(8)]
-        z = cur
-        f = cur
-        for t in range(8):
-            d = jnp.broadcast_to(dc[t][t : t + 1, :], (8, 128))
-            rd = 1.0 / d
-            rs = lax.rsqrt(d)
-            rdn = jnp.concatenate([rd] * (n // 128), axis=1)
-            col = dc[t]
-            zrow = jnp.broadcast_to(z[t : t + 1, :], (8, n)) * rdn
-            coln = jnp.concatenate([col] * (n // 128), axis=1)
-            rsn = jnp.concatenate([rs] * (n // 128), axis=1)
-            f = jnp.where(row == t, f * rsn, jnp.where(row > t, z - coln * zrow, f))
-            z = jnp.where(row == t, zrow, z - coln * zrow)
-            for s in range(t + 1, 8):
-                e = jnp.broadcast_to(dc[s][t : t + 1, :], (8, 128)) * rd
-                dc[s] = jnp.where(row1 == t, e, dc[s] - col * e)
+        dc = [jnp.broadcast_to(z[:, j0 + t : j0 + t + 1], (8, 128)) for t in range(8)]
+        for t in range(0, 8, 2):
+            u = t + 1
+            p, q = dc[t], dc[u]
+            a = jnp.broadcast_to(p[t : t + 1, :], (8, 128))
+            b = jnp.broadcast_to(p[u : u + 1, :], (8, 128))
+            c = jnp.broadcast_to(q[u : u + 1, :], (8, 128))
+            det = a * c - b * b
+            rdet = lax.rsqrt(det)
+            r = rdet * rdet
+            ar, br, cr = a * r, b * r, c * r
+            for s in range(u + 1, 8):
+                et = jnp.broadcast_to(dc[s][t : t + 1, :], (8, 128))
+                eu = jnp.broadcast_to(dc[s][u : u + 1, :], (8, 128))
+                nt, nu = cr * et - br * eu, ar * eu - br * et
+                dc[s] = jnp.where(row1 == t, nt, jnp.where(row1 == u, nu, (dc[s] - p * nt) - q * nu))
+            zt = jnp.broadcast_to(z[t : t + 1, :], (8, n))
+            zu = jnp.broadcast_to(z[u : u + 1, :], (8, n))
+            ra = lax.rsqrt(a)
+            sa = a * ra
+            ba = b * (ra * ra)
+            rd = rdet * sa
+            ft = zt * wide(ra)
+            fu = (zu - wide(ba) * zt) * wide(rd)
+            f = jnp.where(row == t, ft, jnp.where(row == u, fu, f))
+            nt, nu = wide(cr) * zt - wide(br) * zu, wide(ar) * zu - wide(br) * zt
+            z = jnp.where(row == t, nt, jnp.where(row == u, nu, (z - wide(p) * nt) - wide(q) * nu))
         out.append(f)
         for i in range(g + 1, ng):
             acc = w[i]
@@ -341,36 +356,48 @@
     return out
 
 def tail(gram, image, ortho, tri):
-    r8 = lax.broadcasted_iota(jnp.int32, (8, 128), 0)
-    c8 = lax.broadcasted_iota(jnp.int32, (8, 128), 1)
-    eye = [(r8 + 8 * g == c8).astype(F32) for g in range(16)]
-    w = [jnp.concatenate([gram[8 * g : 8 * g + 8, :], eye[g]], axis=1) for g in range(16)]
-    o = jnp.concatenate(factor(w, 384), axis=0)
+    def dot(a, b, ca, cb):
+        return lax.dot_general(a, b, (((ca,), (cb,)), ((), ())), precision=lax.Precision.HIGHEST, preferred_element_type=F32)
+
     rr = lax.broadcasted_iota(jnp.int32, (128, 128), 0)
     cc = lax.broadcasted_iota(jnp.int32, (128, 128), 1)
+    eye = (rr == cc).astype(F32)
     up = cc >= rr
-    u11 = jnp.where(up, o[:, :128], 0.0)
-    u12 = o[:, 128:256]
-    i11 = o[:, 256:]
-    a22 = gram[128:, 128:] - lax.dot_general(u12, u12, (((0,), (0,)), ((), ())), precision=lax.Precision.HIGHEST, preferred_element_type=F32)
-    q1 = lax.dot_general(image[:, :128], i11, (((1,), (1,)), ((), ())), precision=lax.Precision.HIGHEST, preferred_element_type=F32)
-    rest = image[:, 128:] - jnp.dot(q1, u12, precision=lax.Precision.HIGHEST, preferred_element_type=F32)
-    w = [jnp.concatenate([a22[8 * g : 8 * g + 8, :], eye[g]], axis=1) for g in range(16)]
-    o2 = jnp.concatenate(factor(w, 256), axis=0)
-    q2 = lax.dot_general(rest, o2[:, 128:], (((1,), (1,)), ((), ())), precision=lax.Precision.HIGHEST, preferred_element_type=F32)
-    ortho[:, :128] = q1
-    ortho[:, 128:] = q2
-    tri[:128, :128] = u11
-    tri[:128, 128:] = u12
-    tri[128:, :128] = jnp.zeros((128, 128), F32)
-    tri[128:, 128:] = jnp.where(up, o2[:, :128], 0.0)
+    lo, hi = slice(0, 128), slice(128, 256)
+    diag = [gram[q, q] * eye for q in (lo, hi)]
+    across = [jnp.sum(d, axis=0, keepdims=True) for d in diag]
+    down = [lax.rsqrt(jnp.sum(d, axis=1, keepdims=True)) for d in diag]
+    inv = [lax.rsqrt(d) for d in across]
+    root = [d * v for d, v in zip(across, inv)]
+    def groups(*blocks):
+        m = jnp.concatenate(blocks, axis=1)
+        return [m[8 * g : 8 * g + 8, :] for g in range(16)]
+
+    w = groups(gram[lo, lo] * (down[0] * inv[0]), gram[lo, hi] * (down[0] * inv[1]), eye)
+    o = jnp.concatenate(factor(w, 384), axis=0)
+    u12 = o[:, hi]
+    a22 = gram[hi, hi] * (down[1] * inv[1]) - dot(u12, u12, 0, 0)
+    q1 = dot(image[:, lo] * inv[0], o[:, 256:], 1, 1)
+    rest = image[:, hi] * inv[1] - dot(q1, u12, 1, 0)
+    o2 = jnp.concatenate(factor(groups(a22, eye), 256), axis=0)
+    ortho[:, lo] = q1
+    ortho[:, hi] = dot(rest, o2[:, hi], 1, 1)
+    tri[lo, lo] = jnp.where(up, o[:, lo] * root[0], 0.0)
+    tri[lo, hi] = u12 * root[1]
+    tri[hi, lo] = jnp.zeros((128, 128), F32)
+    tri[hi, hi] = jnp.where(up, o2[:, lo] * root[1], 0.0)
+
 
 def orthonormalise(image, gram):
     v = pl.BlockSpec(memory_space=pltpu.VMEM)
-    return pl.pallas_call(tail,
+    return pl.pallas_call(
+        tail,
         out_shape=(jax.ShapeDtypeStruct(image.shape, F32), jax.ShapeDtypeStruct(gram.shape, F32)),
-        in_specs=[v, v], out_specs=(v, v), name="orthonormalise",
-        compiler_params=pltpu.CompilerParams(vmem_limit_bytes=16 * 2**20))(gram, image)
+        in_specs=[v, v],
+        out_specs=(v, v),
+        compiler_params=pltpu.CompilerParams(vmem_limit_bytes=16 * 2**20),
+        name="orthonormalise",
+    )(gram, image)
 
 
 def body(matrix, basis):

time: 94.8 us -> 90.5 us (0.955)
  Pallas kernels: 93.2 us -> 89 us
    pallas_call x1, Pallas kernels: 82.6 us -> 79.3 us  [image_and_gram(): pl.pallas_call(kernel, out_shape=(jax.ShapeDtypeStruct((BLK, KC), F32), j...]
where the time goes in v5:
time: 90.5 us; the launch traced here: 90.4 us
  Pallas kernels  89 us (98%)
    pallas_call x1, Pallas kernels, image_and_gram(): pl.pallas_call(kernel, out_shape=(jax.ShapeDtypeStruct((BLK, KC), F32), j...  79.3 us
    pallas_call x1, Pallas kernels, orthonormalise(): pl.pallas_call(tail, out_shape=(jax.ShapeDtypeStruct(image.shape, F32), j...  9.74 us

profile of v5, /device:TPU:1, one launch (start us, length us, event | category | flops | bytes accessed | tf_op | source)
XLA Modules:
  0.0 90.4 jit_solution(10444755979067176696)
XLA Ops:
  0.6 0.0 copy-start
  0.6 0.7 copy-done
  1.4 79.3 %image_and_gram.1 = (f32[64,256]{1,0:T(8,128)S(1)}, f32[256,256]{1,0:T(8,128)S(1)}) custom-call(bf16[2048,2048]{1,0:T(8,128)(2,1)} %a_hbm.1, bf16[64,256]{1,0:T(8,128)(2,1)S(1)} %copy-done), custom_call_target="tpu_custom_call" | custom-call | flops 8589934592 | bytes 8388608 | tf_op jit(solution)/shard_map/image_and_gram/pallas_call | solution.py:265
  80.6 9.7 %orthonormalise.1 = (f32[64,256]{1,0:T(8,128)}, f32[256,256]{1,0:T(8,128)}) custom-call(f32[256,256]{1,0:T(8,128)S(1)} %get-tuple-element.4.gram, f32[64,256]{1,0:T(8,128)S(1)} %get-tuple-element.5.image), custom_call_target="tpu_custom_call" | custom-call | tf_op jit(solution)/shard_map/orthonormalise/pallas_call | solution.py:393
Async XLA Ops:
  0.6 0.8 copy-start

commit v6 on v5

--- a/solution.py
+++ b/solution.py
@@ -12,6 +12,8 @@
 BLK = 64
 GA = 48
 IA = 48
+ZPOS = (0, 1, 7, 2, 6, 3, 5, 4)
+ZGROUPS = ((0, 5), (5, 8))
 IDT = BF16
 XS = (2, 1, 3, 0)
 XFAR, XNEAR = BF16, F32
@@ -69,7 +71,7 @@
     pl.semaphore_signal(barrier, 1, device_id=at_k())
     first.wait()
     for h in halves:
-        g[h, z, y] = basis[:, 128 * h : 128 * h + 128]
+        g[h, 0, y] = basis[:, 128 * h : 128 * h + 128]
     pl.semaphore_wait(barrier, NZ + NY + NX - 3 + 1)
 
     sends = []
@@ -80,28 +82,37 @@
         sends.append(cp)
         return cp
 
+    def drain(*keep):
+        kept = [cp for group in keep for cp in group]
+        for cp in sends:
+            if all(cp is not other for other in kept):
+                cp.wait_send()
+        sends[:] = kept
+
     hi, lo = pl.ds(0, GA), pl.ds(GA, BLK - GA)
     cy, cz, cyz, czy = {}, {}, {}, {}
     for h in halves:
         k128 = pl.ds(128 * h, 128)
         for s in near:
-            cz[h, s] = copy(basis.at[hi, k128], g.at[h, z, y, hi], s_gz.at[h, s], r_gz.at[h, s], at_z(s))
+            cz[h, s] = copy(
+                basis.at[hi, k128], g.at[h, ZPOS.index(s), y, hi], s_gz.at[h, s], r_gz.at[h, s], at_z(s)
+            )
         for s in (2, 1, 3):
-            cy[h, s] = copy(basis.at[lo, k128], g.at[h, z, y, lo], s_gy.at[h, s], r_gy.at[h, s], at_y(s))
-        for t in (2, 1, 3):
-            czy[h, 0, t] = copy(basis.at[hi, k128], g.at[h, z, y, hi], s_gzy.at[h, 0, t], r_gzy.at[h, 0, t], at_y(t))
+            cy[h, s] = copy(basis.at[lo, k128], g.at[h, 0, y, lo], s_gy.at[h, s], r_gy.at[h, s], at_y(s))
     for h in halves:
         for s in (1, 3, 2):
             cy[h, s].wait_recv()
         for s in far:
-            cyz[h, s] = copy(g.at[h, z, :, lo], g.at[h, z, :, lo], s_gyz.at[h, s], r_gyz.at[h, s], at_z(s))
-        for s in near:
-            cz[h, s].wait_recv()
-            zs = (z + NZ - s) % NZ
+            cyz[h, s] = copy(
+                g.at[h, 0, :, lo], g.at[h, ZPOS.index(s), :, lo], s_gyz.at[h, s], r_gyz.at[h, s], at_z(s)
+            )
+        for q, (first, last) in enumerate(ZGROUPS):
+            for s in ZPOS[first:last]:
+                if s:
+                    cz[h, s].wait_recv()
+            blocks = g.at[h, pl.ds(first, last - first), y, hi]
             for t in (2, 1, 3):
-                czy[h, s, t] = copy(
-                    g.at[h, zs, y, hi], g.at[h, zs, y, hi], s_gzy.at[h, s, t], r_gzy.at[h, s, t], at_y(t)
-                )
+                czy[h, q, t] = copy(blocks, blocks, s_gzy.at[h, q, t], r_gzy.at[h, q, t], at_y(t))
 
     def product(h, j):
         return jnp.dot(bt[h], av[j], preferred_element_type=F32)
@@ -110,12 +121,13 @@
     for h in halves:
         for s in far:
             cyz[h, s].wait_recv()
-        for s in (0, *near):
+        for q in range(len(ZGROUPS)):
             for t in (1, 3, 2):
-                czy[h, s, t].wait_recv()
-
-        for i in range(NZ):
-            bt[h, :, 256 * i : 256 * i + 256] = g[h, i].reshape(NY * BLK, 128).T
+                czy[h, q, t].wait_recv()
+
+        for i, s in enumerate(ZPOS):
+            at = pl.ds(pl.multiple_of(256 * ((z + NZ - s) % NZ), 256), 256)
+            bt[h, :, at] = g[h, i].reshape(NY * BLK, 128).T
         if h == 0:
             for cp in loads:
                 cp.wait()
@@ -133,6 +145,7 @@
                 cx[h, i] = copy(src, dst, s_x.at[h, i], r_x.at[h, i], at_x(s))
             else:
                 own[h] = p
+    drain(cx.values())
     csx, csk = {}, {}
     for h in halves:
         for i in (1, 2, 0):
@@ -143,6 +156,7 @@
         for s in (2, 1, 3):
             csx[h, s] = copy(mine, mine, s_sx.at[h, s], r_sx.at[h, s], at_x(s))
         csk[h, 0] = copy(mine, mine, s_sk.at[h, 0], r_sk.at[h, 0], at_k())
+    drain(csx.values(), csk.values())
 
     nb = BLK - IA
     cya, czb, cza, cyb = {}, {}, {}, {}
@@ -177,6 +191,7 @@
             czb[h, s] = copy(sb.at[h, s], zb.at[h, s], s_zb.at[h, s], r_zb.at[h, s], at_z(s))
         ta[h] = v4[h, :, y, :IA, :]
         ub[h] = v4[h, z, :, IA:, :]
+    drain(cya.values(), czb.values())
     for h in halves:
         for s in (1, 3, 2):
             cya[h, s].wait_recv()
@@ -190,6 +205,7 @@
         ub[h] = u
         for s in (2, 1, 3):
             cyb[h, s] = copy(ub.at[h, (y + s) % NY], yb.at[h, s], s_yb.at[h, s], r_yb.at[h, s], at_y(s))
+    drain(cza.values(), cyb.values())
     scale = 65536.0**-0.5
     for h in halves:
         low = ub[h, y]
@@ -210,6 +226,7 @@
     ) * (1.0 / 16384.0)
     half = pl.multiple_of(128 * k, 128)
     cp = copy(g0.at[pl.ds(pl.multiple_of(128 * (1 - k), 128), 128)], gk, s_q.at[0], r_q.at[0], at_k())
+    drain([cp])
     cp.wait_recv()
     g1[...] = g0[pl.ds(half, 128), :] + gk[...]
 
@@ -222,6 +239,7 @@
         piece = g1.at[rows8((x + s) % NX, (y + t) % NY)]
         cps.append(copy(piece, gx.at[q], s_q.at[q], r_q.at[q], at_xy(s, t)))
     acc = g1[rows8(x, y), :]
+    drain(cps)
     for (s, t), cp in zip(reversed(shifts), reversed(cps)):
         cp.wait_recv()
     for s, t in shifts:
@@ -230,6 +248,7 @@
     cps = []
     for s in far:
         cps.append(copy(gz.at[z], gz.at[z], s_q.at[15 + s], r_q.at[15 + s], at_z(s)))
+    drain(cps)
     for cp in cps:
         cp.wait_recv()
     row8 = pl.ds(pl.multiple_of(half + 32 * x + 8 * y, 8), 8)
@@ -238,6 +257,7 @@
     for s, t in sorted(shifts, key=lambda v: -min(v[0], NX - v[0]) - min(v[1], NY - v[1])):
         q = 23 + NY * s + t
         cps[s, t] = copy(gf.at[row8], gf.at[row8], s_q.at[q], r_q.at[q], at_xy(s, t))
+    drain(cps.values())
     ckf = []
     for s in (0, 1, 3, 2):
         for t in range(NY):
@@ -248,8 +268,7 @@
     for cp in ckf:
         cp.wait_recv()
     gram_out[...] = gf[...]
-    for cp in sends:
-        cp.wait_send()
+    drain()
 
 
 def image_and_gram(matrix, basis):
@@ -257,7 +276,7 @@
     nb = BLK - IA
     sems = []
     for shape in (
-        (2, NZ), (2, NZ, NY), (2, NY), (2, NZ),
+        (2, NZ), (2, 2, NY), (2, NY), (2, NZ),
         (2, 4), (2, 3), (2, 4), (2, 4),
         (2, NY), (2, NZ), (2, NZ), (2, NY), (43,),
     ):

time: 90.5 us -> 90.8 us (level)
  no operation moved by 1% of the time
where the time goes in v6:
time: 90.8 us; the launch traced here: 90.6 us
  Pallas kernels  89.2 us (98%)
    pallas_call x1, Pallas kernels, image_and_gram(): pl.pallas_call(kernel, out_shape=(jax.ShapeDtypeStruct((BLK, KC), F32), j...  79.5 us
    pallas_call x1, Pallas kernels, orthonormalise(): pl.pallas_call(tail, out_shape=(jax.ShapeDtypeStruct(image.shape, F32), j...  9.74 us

profile of v6, /device:TPU:1, one launch (start us, length us, event | category | flops | bytes accessed | tf_op | source)
XLA Modules:
  0.0 90.6 jit_solution(7048087601174795583)
XLA Ops:
  0.6 0.0 copy-start
  0.6 0.7 copy-done
  1.4 79.5 %image_and_gram.1 = (f32[64,256]{1,0:T(8,128)S(1)}, f32[256,256]{1,0:T(8,128)S(1)}) custom-call(bf16[2048,2048]{1,0:T(8,128)(2,1)} %a_hbm.1, bf16[64,256]{1,0:T(8,128)(2,1)S(1)} %copy-done), custom_call_target="tpu_custom_call" | custom-call | flops 8589934592 | bytes 8388608 | tf_op jit(solution)/shard_map/image_and_gram/pallas_call | solution.py:284
  80.9 9.7 %orthonormalise.1 = (f32[64,256]{1,0:T(8,128)}, f32[256,256]{1,0:T(8,128)}) custom-call(f32[256,256]{1,0:T(8,128)S(1)} %get-tuple-element.4.gram, f32[64,256]{1,0:T(8,128)S(1)} %get-tuple-element.5.image), custom_call_target="tpu_custom_call" | custom-call | tf_op jit(solution)/shard_map/orthonormalise/pallas_call | solution.py:412
Async XLA Ops:
  0.6 0.8 copy-start
